TPU v7x, 32 devices: a whole 2x2x4 slice. The times are simulated.
32 devices in a mesh: visit: 8 (over y, x, core), ccd: 4 (over z).
Axes of the slice: x: 2, y: 2, z: 4, core: 2. Of those that a mesh axis runs over, the one named last changes fastest.
Arguments:
- raw_rows: bfloat16 [32, 4096, 128], P('visit', 'ccd')
- resample: bfloat16 [32, 128, 128], P('visit')
- slot_row: int32 [8, 4, 8, 128], P('visit', 'ccd'), may hold values from 0 to 4092, as said below
- tap_weight: float32 [4, 8, 4, 8, 128], P(None, 'visit', 'ccd'), may hold values from 0 to 1
- patch_id: int32 [8, 4, 8, 128], P('visit', 'ccd'), may hold values from 0 to 15
- live_mask: int32 [8, 4, 8, 128], P('visit', 'ccd'), may hold values 0 or 1
Outputs:
- offsets: float32 [32, 64], P('visit')
- background: float32 [512, 128], P(('visit', 'ccd'))
Inputs may be any that keep to these rules, and one draw needn't show every extreme that they name: `slot_row`: each value is v * 1024 + b with v below 4 and b at most 1020.
All inputs are finite; a program needn't handle non-finite values. No bound on the sum of `live_mask` on one device may be relied on, other than what follows from the above.
Results may differ from a plain program's by a relative error of at most 0.0041.
Values may be sent and summed in bfloat16 or wider, within the bound.
A program may use at most 64 MiB of HBM per device.

v0:
```python
import jax
import jax.numpy as jnp
from jax import lax
from jax.sharding import PartitionSpec as P

ORDER = 8
TAPS = 4
ITERS = 2
P_DEV = 16


ridge_weight = 1.0


def chebyshev(coords):
    series = [jnp.ones_like(coords), coords]
    for degree in range(2, ORDER):
        series.append(2.0 * coords * series[-1] - series[-2])
    return jnp.stack(series[:ORDER])


def model_of(coef_rows, cheb_rows, cheb_x):
    shaped = coef_rows.reshape(coef_rows.shape[:-1] + (ORDER, ORDER))
    reduced = jnp.sum(shaped * cheb_rows[..., None, :], axis=-1)
    return jnp.einsum("...i,ip->...p", reduced, cheb_x, precision=lax.Precision.HIGHEST)


def solve_offsets(gram_x, design, moments):
    design_sq = design.reshape(-1, ORDER, ORDER)
    gram = jnp.einsum("ac,vbd->vabcd", gram_x, design_sq).reshape(-1, ORDER * ORDER, ORDER * ORDER)
    gram = gram + ridge_weight * jnp.eye(ORDER * ORDER, dtype=jnp.float32)
    factor = jnp.linalg.cholesky(gram)
    return jax.scipy.linalg.cho_solve((factor, True), moments[..., None])[..., 0]


def consensus(arrived, sweep_codes):
    patch_hot = (sweep_codes[..., None] == jnp.arange(P_DEV, dtype=jnp.int32)).astype(jnp.bfloat16)
    counts = jnp.sum(patch_hot.astype(jnp.float32), axis=(0, 1))
    sums = jnp.einsum("nsk,nsq->kq", patch_hot, arrived, preferred_element_type=jnp.float32)
    background = sums / (counts + 1.0)[:, None]
    returned = jnp.einsum(
        "nsk,kq->nsq",
        patch_hot,
        background.astype(jnp.bfloat16),
        preferred_element_type=jnp.float32,
    ).astype(jnp.bfloat16)
    return (background, returned)


def per_device(raw_rows, resample, slot_row, tap_weight, patch_id, live_mask):
    f32 = jnp.float32
    visit_devs = lax.axis_size("visit")
    ccd_devs = lax.axis_size("ccd")
    ccd_index = lax.axis_index("ccd")
    vis_local, rows_local, pixels = raw_rows.shape
    slots = slot_row.shape[3]
    resampled = jnp.einsum("vrp,vpq->vrq", raw_rows, resample, preferred_element_type=f32)
    resampled = resampled.reshape(vis_local * rows_local, pixels)
    starts = slot_row[0, 0]
    weights = tap_weight[:, 0, 0]
    blended = jnp.zeros((visit_devs, slots, pixels), f32)
    for tap_index in range(TAPS):
        blended = blended + weights[tap_index][..., None] * jnp.take(
            resampled, starts + tap_index, axis=0
        )
    warped = blended.astype(jnp.bfloat16)
    local_visit = starts // rows_local
    row_pos = ccd_index * rows_local + starts % rows_local
    coord_y = (2 * row_pos + TAPS).astype(f32) / float(rows_local * ccd_devs) - 1.0
    cheb_y = jnp.moveaxis(chebyshev(coord_y), 0, -1)
    cheb_x = chebyshev((2 * jnp.arange(pixels) + 1).astype(f32) / float(pixels) - 1.0)
    gram_x = jnp.dot(cheb_x, cheb_x.T, precision=lax.Precision.HIGHEST)
    live_float = live_mask[0, 0].astype(f32)
    codes = patch_id[0, 0] + P_DEV * (1 - live_mask[0, 0])
    visit_hot = (local_visit[..., None] == jnp.arange(vis_local, dtype=jnp.int32)).astype(f32)
    visit_hot = visit_hot.reshape(-1, vis_local)
    outer_y = cheb_y[..., :, None] * cheb_y[..., None, :] * live_float[..., None, None]
    design_local = jnp.dot(
        visit_hot.T, outer_y.reshape(-1, ORDER * ORDER), precision=lax.Precision.HIGHEST
    )
    offset_coefs = jnp.zeros((vis_local, ORDER * ORDER), f32)
    background = jnp.zeros((P_DEV, pixels), f32)
    for sweep in range(ITERS):
        model = model_of(jnp.take(offset_coefs, local_visit, axis=0), cheb_y, cheb_x)
        corrected = (warped.astype(f32) - model).astype(jnp.bfloat16)
        arrived, sweep_codes = (
            lax.all_to_all(corrected, "visit", split_axis=0, concat_axis=0, tiled=True),
            lax.all_to_all(codes, "visit", split_axis=0, concat_axis=0, tiled=True),
        )
        background, returned = consensus(arrived, sweep_codes)
        matched = lax.all_to_all(returned, "visit", split_axis=0, concat_axis=0, tiled=True)
        resid = (warped.astype(f32) - matched.astype(f32)) * live_float[..., None]
        projected = jnp.einsum("nsp,ip->nsi", resid, cheb_x, precision=lax.Precision.HIGHEST)
        moment_rows = (projected[..., :, None] * cheb_y[..., None, :]).reshape(-1, ORDER * ORDER)
        moments_local = jnp.dot(visit_hot.T, moment_rows, precision=lax.Precision.HIGHEST)
        design_total, moments = lax.psum((design_local, moments_local), "ccd")
        offset_coefs = solve_offsets(gram_x, design_total, moments)
    return (offset_coefs, background)


def solution(mesh):
    in_specs = (
        P("visit", "ccd", None),
        P("visit", None, None),
        P("visit", "ccd", None, None),
        P(None, "visit", "ccd", None, None),
        P("visit", "ccd", None, None),
        P("visit", "ccd", None, None),
    )
    out_specs = (P("visit", None), P(("visit", "ccd"), None))
    return jax.shard_map(
        per_device, mesh=mesh, in_specs=in_specs, out_specs=out_specs, check_vma=False
    )
```

profile of v0, /device:TPU:0, one launch (start us, length us, event | category | flops | bytes accessed | tf_op | source)
XLA Modules:
  0.0 158.0 jit_solution(10821728541467302561)
XLA Ops:
  0.6 1.4 convert_bitcast_fusion.1
  2.0 5.2 %all-to-all-start = ((s32[8,1,128]{2,1,0:T(1,128)}), s32[8,1,128]{2,1,0:T(1,128)S(1)}, u32[]{:S(2)}, u32[]{:S(2)}) async-start(s32[8,1,128]{2,1,0:T(1,128)} %bitcast.23), calls=%async_computation | async-start | bytes 8192 | tf_op jit(solution)/shard_map/all_to_all | solution.py:88
  7.2 0.7 add_select_fusion.3
  7.9 0.7 compare_and_fusion
  9.2 1.3 fusion.76
  10.6 4.0 %gather_fusion = f32[1024,128]{1,0:T(8,128)} fusion(f32[4096,128]{1,0:T(8,128)S(1)} %bitcast.249, s32[1024]{0:T(1024)S(1)} %get-tuple-element.22), kind=kCustom, calls=%fused_computation.clone | custom fusion | bytes 1052672 | tf_op jit(solution)/shard_map/jit(_take)/gather | solution.py:63
  14.5 4.0 %gather_fusion.1 = f32[1024,128]{1,0:T(8,128)} fusion(f32[4096,128]{1,0:T(8,128)S(1)} %bitcast.250, s32[1024]{0:T(1024)S(1)} %get-tuple-element.18), kind=kCustom, calls=%fused_computation.2.clone | custom fusion | bytes 1052672 | tf_op jit(solution)/shard_map/jit(_take)/gather | solution.py:63
  18.5 4.0 %gather_fusion.2 = f32[1024,128]{1,0:T(8,128)} fusion(f32[4096,128]{1,0:T(8,128)S(1)} %bitcast.251, s32[1024]{0:T(1024)S(1)} %get-tuple-element.21), kind=kCustom, calls=%fused_computation.3.clone | custom fusion | bytes 1052672 | tf_op jit(solution)/shard_map/jit(_take)/gather | solution.py:63
  22.5 4.0 %gather_fusion.3 = f32[1024,128]{1,0:T(8,128)} fusion(f32[4096,128]{1,0:T(8,128)S(1)} %bitcast.252, s32[1024]{0:T(1024)S(1)} %get-tuple-element.19), kind=kCustom, calls=%fused_computation.4.clone | custom fusion | bytes 1052672 | tf_op jit(solution)/shard_map/jit(_take)/gather | solution.py:63
  26.7 2.8 %gather_fusion.4 = f32[1024,64]{1,0:T(8,128)S(1)} fusion(f32[4,64]{1,0:T(4,128)S(1)} %broadcast_in_dim.26, s32[1024]{0:T(1024)S(1)} %get-tuple-element.20), kind=kCustom, calls=%fused_computation.1.clone | custom fusion | bytes 528384 | tf_op jit(solution)/shard_map/jit(_take)/gather | solution.py:84
  29.9 0.7 stack.5
  30.6 2.9 %fusion.13 = bf16[8,128,128]{2,1,0:T(8,128)(2,1)S(1)} fusion(f32[8,128,128]{2,1,0:T(8,128)} %bitcast.258, f32[8,128,128]{2,1,0:T(8,128)S(1)} %bitcast.257, f32[8,128,128]{2,1,0:T(8,128)S(1)} %bitcast.256, f32[8,128,128]{2,1,0:T(8,128)S(1)} %bitcast.255, f32[8,128]{1,0:T(8,128)S(1)} %get-tuple-element.12, f32[8,128]{1,0:T(8,128)S(1)} %get-tuple-element.13, ...), kind=kLoop, calls=%fused_computation.31 | loop fusion | flops 1572864 | bytes 2379776 | tf_op jit(solution)/shard_map/convert_element_type | solution.py:66
  33.5 1.7 %fusion = bf16[8,128,128]{2,1,0:T(8,128)(2,1)} fusion(f32[8,128,8]{1,2,0:T(8,128)S(1)} %fusion.29, bf16[8,128,128]{2,1,0:T(8,128)(2,1)S(1)} %fusion.13, f32[8,128]{1,0:T(8,128)S(1)} %stack.5), kind=kOutput, calls=%fused_computation.10 | convolution fusion | flops 12976128 | bytes 561152 | tf_op jit(solution)/shard_map/...i,ip->...p/dot_general | solution.py:25
  35.2 4.2 %all-to-all-start.1 = ((bf16[8,128,128]{2,1,0:T(8,128)(2,1)}), bf16[8,128,128]{2,1,0:T(8,128)(2,1)S(1)}, u32[]{:S(2)}, u32[]{:S(2)}) async-start(bf16[8,128,128]{2,1,0:T(8,128)(2,1)} %fusion), calls=%async_computation.1 | async-start | bytes 524288 | tf_op jit(solution)/shard_map/all_to_all | solution.py:87
  39.5 6.8 %all-to-all-done.1 = bf16[8,128,128]{2,1,0:T(8,128)(2,1)S(1)} async-done(((bf16[8,128,128]{2,1,0:T(8,128)(2,1)}), bf16[8,128,128]{2,1,0:T(8,128)(2,1)S(1)}, u32[]{:S(2)}, u32[]{:S(2)}) %all-to-all-start.1) | async-done | bytes 262176 | tf_op jit(solution)/shard_map/all_to_all | solution.py:87
  46.3 1.1 convolution_convert_fusion.1
  47.4 3.4 %all-to-all-start.2 = ((bf16[8,128,128]{2,1,0:T(8,128)(2,1)}), bf16[8,128,128]{2,1,0:T(8,128)(2,1)S(1)}, u32[]{:S(2)}, u32[]{:S(2)}) async-start(bf16[8,128,128]{2,1,0:T(8,128)(2,1)} %convolution_convert_fusion.1), calls=%async_computation.2 | async-start | bytes 524288 | tf_op jit(solution)/shard_map/all_to_all | solution.py:91
  50.9 6.7 %all-to-all-done.2 = bf16[8,128,128]{2,1,0:T(8,128)(2,1)S(1)} async-done(((bf16[8,128,128]{2,1,0:T(8,128)(2,1)}), bf16[8,128,128]{2,1,0:T(8,128)(2,1)S(1)}, u32[]{:S(2)}, u32[]{:S(2)}) %all-to-all-start.2) | async-done | bytes 262176 | tf_op jit(solution)/shard_map/all_to_all | solution.py:91
  57.7 0.7 fusion.7
  58.6 0.6 fusion.21
  59.4 0.6 convolution_bitcast_fusion.3
  60.0 19.2 %all-reduce = (f32[4,64,1]{1,0,2:T(4,128)S(1)}, f32[4,8,8]{2,1,0:T(8,128)S(1)}) all-reduce(f32[4,64,1]{1,0,2:T(4,128)S(1)} %convolution_bitcast_fusion.3, f32[4,8,8]{2,1,0:T(8,128)S(1)} %reshape.398), channel_id=1, replica_groups=mesh['visit'=8,'ccd'=4] {'ccd'}, use_global_device_ids=true, to_apply=%region_5.9 | all-reduce | flops 512 | bytes 4096 | tf_op jit(solution)/shard_map/psum | solution.py:96
  79.9 23.5 %custom-call.9 = f32[4,64,64]{2,1,0:T(8,128)S(1)} custom-call(f32[4,64,64]{2,1,0:T(8,128)S(1)} %fusion.41), custom_call_target="Cholesky" | custom-call | tf_op jit(solution)/shard_map/jit(cholesky)/cholesky | solution.py:32
  103.6 19.7 %custom-call.11 = f32[4,1,64,64]{2,3,1,0:T(8,128)S(1)} custom-call(f32[4,1,64,64]{3,2,1,0:T(8,128)S(1)} %select_bitcast_fusion), custom_call_target="InvertDiagBlocksLowerTriangular" | custom-call | tf_op jit(solution)/shard_map/jit(_cho_solve)/vmap()/triangular_solve | solution.py:33
  123.8 2.8 %gather_fusion.5 = f32[1024,64]{1,0:T(8,128)S(1)} fusion(f32[4,64]{1,0:T(4,128)S(1)} %bitcast.248, s32[1024]{0:T(1024)S(1)} %get-tuple-element.20), kind=kCustom, calls=%fused_computation.5.clone | custom fusion | bytes 528384 | tf_op jit(solution)/shard_map/jit(_take)/gather | solution.py:84
  126.9 1.0 fusion.1
  127.9 9.3 %all_to_all.27 = bf16[8,128,128]{2,1,0:T(8,128)(2,1)S(1)} all-to-all(bf16[8,128,128]{2,1,0:T(8,128)(2,1)S(1)} %fusion.1), channel_id=1, replica_groups=mesh['visit'=8,'ccd'=4] {'visit'}, dimensions={0} | all-to-all | bytes 524288 | tf_op jit(solution)/shard_map/all_to_all | solution.py:87
  137.7 9.3 %all_to_all.28 = bf16[8,128,128]{2,1,0:T(8,128)(2,1)S(1)} all-to-all(bf16[8,128,128]{2,1,0:T(8,128)(2,1)S(1)} %convolution_convert_fusion), channel_id=1, replica_groups=mesh['visit'=8,'ccd'=4] {'visit'}, dimensions={0} | all-to-all | bytes 524288 | tf_op jit(solution)/shard_map/all_to_all | solution.py:91
  147.1 0.7 fusion.10
  148.0 0.6 convolution_bitcast_fusion.2
  148.5 8.4 %psum.26 = f32[4,64,1]{1,0,2:T(4,128)S(1)} all-reduce(f32[4,64,1]{1,0,2:T(4,128)S(1)} %convolution_bitcast_fusion.2), channel_id=1, replica_groups=mesh['visit'=8,'ccd'=4] {'ccd'}, use_global_device_ids=true, to_apply=%region_7.12 | all-reduce | flops 256 | bytes 2048 | tf_op jit(solution)/shard_map/psum | solution.py:96
  157.1 0.9 fusion.38
  (61 shorter events, 4.4 us)
Async XLA Ops:
  0.6 8.6 %copy-start = (bf16[4,1024,128]{2,1,0:T(8,128)(2,1)S(1)}, bf16[4,1024,128]{2,1,0:T(8,128)(2,1)}, u32[]{:S(2)}) copy-start(bf16[4,1024,128]{2,1,0:T(8,128)(2,1)} %param.13) | copy-start | bytes 3145732
  2.0 33.1 %all-to-all-start = ((s32[8,1,128]{2,1,0:T(1,128)}), s32[8,1,128]{2,1,0:T(1,128)S(1)}, u32[]{:S(2)}, u32[]{:S(2)}) async-start(s32[8,1,128]{2,1,0:T(1,128)} %bitcast.23), calls=%async_computation | async-start | bytes 8192 | tf_op jit(solution)/shard_map/all_to_all | solution.py:88
  22.5 4.0 %copy-start.5 = (f32[4,1,1,8,128]{4,3,2,1,0:T(8,128)S(1)}, f32[4,1,1,8,128]{4,3,2,1,0:T(8,128)}, u32[]{:S(2)}) copy-start(f32[4,1,1,8,128]{4,3,2,1,0:T(8,128)} %param.16) | copy-start | bytes 49156
  22.5 4.0 %copy-start.4 = (s32[1,1,8,128]{3,2,1,0:T(8,128)S(1)}, s32[1,1,8,128]{3,2,1,0:T(8,128)}, u32[]{:S(2)}) copy-start(s32[1,1,8,128]{3,2,1,0:T(8,128)} %param.15) | copy-start | bytes 12292
  26.7 3.8 %copy-start.1 = (f32[1024,128]{1,0:T(8,128)S(1)}, f32[1024,128]{1,0:T(8,128)}, u32[]{:S(2)}) copy-start(f32[1024,128]{1,0:T(8,128)} %gather_fusion) | copy-start | bytes 1572868
  26.7 3.8 %copy-start.2 = (f32[1024,128]{1,0:T(8,128)S(1)}, f32[1024,128]{1,0:T(8,128)}, u32[]{:S(2)}) copy-start(f32[1024,128]{1,0:T(8,128)} %gather_fusion.1) | copy-start | bytes 1572868
  26.7 3.8 %copy-start.3 = (f32[1024,128]{1,0:T(8,128)S(1)}, f32[1024,128]{1,0:T(8,128)}, u32[]{:S(2)}) copy-start(f32[1024,128]{1,0:T(8,128)} %gather_fusion.2) | copy-start | bytes 1572868
  35.2 11.1 %all-to-all-start.1 = ((bf16[8,128,128]{2,1,0:T(8,128)(2,1)}), bf16[8,128,128]{2,1,0:T(8,128)(2,1)S(1)}, u32[]{:S(2)}, u32[]{:S(2)}) async-start(bf16[8,128,128]{2,1,0:T(8,128)(2,1)} %fusion), calls=%async_computation.1 | async-start | bytes 524288 | tf_op jit(solution)/shard_map/all_to_all | solution.py:87
  47.4 10.3 %all-to-all-start.2 = ((bf16[8,128,128]{2,1,0:T(8,128)(2,1)}), bf16[8,128,128]{2,1,0:T(8,128)(2,1)S(1)}, u32[]{:S(2)}, u32[]{:S(2)}) async-start(bf16[8,128,128]{2,1,0:T(8,128)(2,1)} %convolution_convert_fusion.1), calls=%async_computation.2 | async-start | bytes 524288 | tf_op jit(solution)/shard_map/all_to_all | solution.py:91
  137.4 20.6 %copy-start.6 = (f32[16,128]{1,0:T(8,128)}, f32[16,128]{1,0:T(8,128)S(1)}, u32[]{:S(2)}) copy-start(f32[16,128]{1,0:T(8,128)S(1)} %fusion.2) | copy-start | bytes 24580
where the time goes:
time: 159 us; the launch traced here: 158 us
  other arithmetic  50.4 us (32%)
  blocking collectives  46.2 us (29%)
  local copies, waits for them, and re-layouts  23.7 us (15%)
  waiting for transfers between devices  13.5 us (8%)
  starting transfers between devices  12.8 us (8%)
  matrix products  10.4 us (7%)
    psum x2, blocking collectives, per_device(): design_total, moments = lax.psum((design_local, moments_local), 'ccd')  27.5 us
    another operation x4, other arithmetic, solve_offsets(): factor = jnp.linalg.cholesky(gram)  23.6 us
    another operation x3, other arithmetic, solve_offsets(): jax.scipy.linalg.cho_solve((factor, True), moments[..., None])[..., 0]  19.8 us
    gather x4, local copies, waits for them, and re-layouts, per_device(): jnp.take(resampled, starts + tap_index, axis=0)  16 us
    all_to_all x1, blocking collectives, per_device(): lax.all_to_all(returned, 'visit', split_axis=0, concat_axis=0, tiled=True)  9.35 us
    all_to_all x1, blocking collectives, per_device(): lax.all_to_all(corrected, 'visit', split_axis=0, concat_axis=0, tiled=True)  9.35 us
    all_to_all x1, waiting for transfers between devices, per_device(): lax.all_to_all(corrected, 'visit', split_axis=0, concat_axis=0, tiled=True)  6.81 us
    all_to_all x1, waiting for transfers between devices, per_device(): lax.all_to_all(returned, 'visit', split_axis=0, concat_axis=0, tiled=True)  6.72 us
  transfers between devices with their start and end apart: 3, of which 2 were waited for; matrix products, arithmetic and copies ran while one was open for 18% of the time, Pallas kernels for 0%

commit v1 on v0

v1 whole, which is shorter than its diff:
```python
import functools
import jax
import jax.numpy as jnp
import numpy as np
from jax import lax
from jax.experimental import pallas as pl
from jax.experimental.pallas import tpu as pltpu
from jax.sharding import PartitionSpec as P

ORDER = 8
TAPS = 4
P_DEV = 16
LANES = 128
ROW_BLOCK = 256

ridge_weight = 1.0

MESH = pl.DeviceIdType.MESH
HIGH = lax.Precision.HIGHEST
F32 = jnp.float32
BF16 = jnp.bfloat16
NT = (((1,), (1,)), ((), ()))
NN = (((1,), (0,)), ((), ()))


def basis_constants(pixels, vis_local):
    coord = (2 * np.arange(pixels) + 1) / pixels - 1.0
    rows = [np.ones_like(coord), coord]
    for _ in range(2, ORDER):
        rows.append(2.0 * coord * rows[-1] - rows[-2])
    cheb = np.stack(rows)
    lam, vec = np.linalg.eigh(cheb @ cheb.T)
    used = np.arange(LANES) < vis_local * ORDER
    term = np.arange(LANES) % ORDER
    fold = (term[None] == np.arange(ORDER)[:, None]) * used
    unrot = vec[:, term] * used
    lam_lane = np.broadcast_to(lam[term] * used, (ORDER, LANES))
    wide = np.zeros((4 * ORDER, pixels))
    wide[:ORDER] = vec.T @ cheb
    wide[ORDER : 2 * ORDER, :LANES] = fold
    wide[2 * ORDER : 3 * ORDER, :LANES] = unrot
    wide[3 * ORDER :, :LANES] = lam_lane
    return wide.astype(np.float32)


def dot(a, b, dims, precision=None):
    return lax.dot_general(a, b, dims, precision=precision, preferred_element_type=F32)


def split(x, parts):
    out = []
    for _ in range(parts):
        head = x.astype(BF16)
        out.append(head)
        x = x - head.astype(F32)
    return out


def iota(shape, dim):
    return lax.broadcasted_iota(jnp.int32, shape, dim)


def kernel(
    n_v, n_c, vis_local,
    slot_ref, tap_ref, patch_ref, live_ref, const_ref, raw_hbm, res_hbm,
    off_ref, bg_ref,
    raw_ref, res_ref, iscr, tscr, wscr, tw_ref, d_ref, s_ref, sext_ref, s1_ref,
    pa_ref, q_ref, s_recv, m_recv, m2_recv, pa_recv, q_recv, s1_recv,
    load_sem, ssend, srecv, asend, arecv, bsend, brecv, csend, crecv, dsend, drecv, gsend, grecv,
):
    vi, ci = lax.axis_index("visit"), lax.axis_index("ccd")
    rows = raw_ref.shape[1]
    slots = slot_ref.shape[1]
    npk = n_v * P_DEV
    nvb = vis_local * ORDER
    v_peer = lambda step: (lax.rem(vi + step, n_v), ci)
    c_peer = lambda step: (vi, lax.rem(ci + step, n_c))

    barrier = pltpu.get_barrier_semaphore()
    for step in range(1, n_v):
        pl.semaphore_signal(barrier, inc=1, device_id=v_peer(step), device_id_type=MESH)
    for step in range(1, n_c):
        pl.semaphore_signal(barrier, inc=1, device_id=c_peer(step), device_id_type=MESH)
    raw_load = pltpu.make_async_copy(raw_hbm, raw_ref, load_sem.at[0])
    raw_load.start()
    res_load = pltpu.make_async_copy(res_hbm, res_ref, load_sem.at[1])
    res_load.start()

    def over_visits(src_of, dst, send, recv):
        copies = []
        for step in range(1, n_v):
            copy = pltpu.make_async_remote_copy(
                src_ref=src_of(step), dst_ref=dst.at[step],
                send_sem=send.at[step], recv_sem=recv.at[step],
                device_id=v_peer(step), device_id_type=MESH,
            )
            copy.start()
            copies.append(copy)
        return copies

    def over_ccd(buf, send, recv):
        copies = []
        for step in range(1, n_c):
            copy = pltpu.make_async_remote_copy(
                src_ref=buf.at[ci], dst_ref=buf.at[ci],
                send_sem=send.at[step], recv_sem=recv.at[ci],
                device_id=c_peer(step), device_id_type=MESH,
            )
            copy.start()
            copies.append(copy)
        return copies

    def total_over_ccd(buf, send, recv):
        for step in range(1, n_c):
            sender = lax.rem(ci + n_c - step, n_c)
            pltpu.make_async_remote_copy(
                src_ref=buf.at[sender], dst_ref=buf.at[sender],
                send_sem=send.at[step], recv_sem=recv.at[sender],
                device_id=c_peer(step), device_id_type=MESH,
            ).wait_recv()
        total = buf[0]
        for c in range(1, n_c):
            total = total + buf[c]
        return total

    start = slot_ref[...]
    vis = jnp.zeros_like(start)
    for v in range(1, vis_local):
        vis = vis + (start >= v * rows).astype(jnp.int32)
    base = start - vis * rows
    live = live_ref[...] > 0
    patch = patch_ref[...]
    iscr[0] = jnp.where(live, vis * P_DEV + patch, -1)
    iscr[1] = base
    iscr[2] = jnp.where(live, iota(start.shape, 0) * P_DEV + patch, -1)
    iscr[3] = jnp.where(live, vis, -1)
    coord = (2 * (ci * rows + base) + TAPS).astype(F32) / float(rows * n_c) - 1.0
    older, newer = jnp.ones_like(coord), coord
    for degree in range(2 * ORDER):
        tscr[:, degree, :] = older
        older, newer = newer, 2.0 * coord * newer - older

    tw_ref[...] = jnp.zeros_like(tw_ref)
    d_ref[...] = jnp.zeros_like(d_ref)
    s_ref[...] = jnp.zeros_like(s_ref)
    row_at = iota((ROW_BLOCK, slots), 0)

    def chunk(j, carry):
        at = pl.ds(j, 1)
        first = iscr[1, at, :]
        vis_j = iscr[3, at, :]
        weights = [tap_ref[t, at, :] for t in range(TAPS)]
        cheb = tscr[j]
        hot = jnp.where(iota((vis_local * P_DEV, slots), 0) == iscr[0, at, :], 1.0, 0.0).astype(BF16)
        cheb_v = jnp.concatenate(
            [jnp.where(vis_j == v, cheb[:ORDER], 0.0) for v in range(vis_local)], axis=0
        )
        tv = split(cheb_v, 3)
        lhs = jnp.concatenate([hot, tv[0], tv[1]], axis=0)
        hots = vis_local * P_DEV
        for block in range(0, rows, ROW_BLOCK):
            gap = row_at - (first - block)
            taps = jnp.zeros((ROW_BLOCK, slots), F32)
            for t in range(TAPS):
                taps = jnp.where(gap == t, weights[t], taps)
            prod = dot(lhs, taps.astype(BF16), NT)
            for v in range(vis_local):
                wscr[v, pl.ds(pl.multiple_of(j * P_DEV, P_DEV), P_DEV), block : block + ROW_BLOCK] = (
                    prod[v * P_DEV : (v + 1) * P_DEV].astype(BF16)
                )
            tw_ref[:, block : block + ROW_BLOCK] += prod[hots : hots + nvb] + prod[hots + nvb :]
        member = jnp.where(iota((npk, slots), 0) == iscr[2, at, :], 1.0, 0.0).astype(BF16)
        design = dot(jnp.concatenate(tv, axis=0), member, NT)
        d_ref[...] += design[:nvb] + design[nvb : 2 * nvb] + design[2 * nvb :]
        of_visit = jnp.where((iota((LANES, slots), 0) >> 3) == vis_j, 1.0, 0.0).astype(BF16)
        sums = dot(jnp.concatenate(split(cheb, 3), axis=0), of_visit, NT)
        s_ref[...] += sums[: 2 * ORDER] + sums[2 * ORDER : 4 * ORDER] + sums[4 * ORDER :]
        return carry

    lax.fori_loop(0, n_v, chunk, 0)

    pl.semaphore_wait(barrier, n_v + n_c - 2)
    s_recv[ci] = s_ref[...]
    sent_s = over_ccd(s_recv, ssend, srecv)

    raw_load.wait()
    res_load.wait()
    tw = jnp.concatenate(split(tw_ref[...], 2), axis=0)
    sums1 = jnp.zeros((npk, raw_ref.shape[2]), F32)
    row_sums = []
    for v in range(vis_local):
        by_patch = dot(wscr[v], raw_ref[v], NN)
        by_term = dot(tw, raw_ref[v], NN)
        by_term = (by_term[:nvb] + by_term[nvb:])[v * ORDER : (v + 1) * ORDER]
        mixed = jnp.concatenate([by_patch, by_term, jnp.zeros_like(by_term)], axis=0)
        high, low = split(mixed, 2)
        warped = dot(high, res_ref[v], NN) + dot(low, res_ref[v], NN)
        sums1 = sums1 + warped[:npk]
        row_sums.append(warped[npk : npk + ORDER])
    s1_ref[...] = sums1
    cx = const_ref[:ORDER]
    design = d_ref[...]
    count = jnp.zeros((1, npk), F32)
    for v in range(vis_local):
        count = count + design[v * ORDER : v * ORDER + 1]
    pa_ref[:ORDER] = dot(cx, sums1, NT, HIGH)
    pa_ref[ORDER:] = jnp.broadcast_to(count, (ORDER, npk))
    sent_a = over_visits(lambda step: pa_ref, pa_recv, asend, arecv)

    def owner_rows(step):
        owner = lax.rem(vi + step, n_v)
        return s1_ref.at[pl.ds(pl.multiple_of(owner * P_DEV, P_DEV), P_DEV)]

    sent_g = over_visits(owner_rows, s1_recv, gsend, grecv)

    lane_visit = iota((ORDER, LANES), 1) >> 3

    def own_blocks(full):
        total = jnp.zeros((ORDER, LANES), F32)
        for v in range(vis_local):
            total = total + jnp.where(lane_visit == v, full[v * ORDER : (v + 1) * ORDER], 0.0)
        return total

    def repeat(x):
        return jnp.concatenate([x] * (LANES // ORDER), axis=0)

    warped_moment = own_blocks(dot(jnp.concatenate(row_sums, axis=0), repeat(cx), NT, HIGH))

    s_total = total_over_ccd(s_recv, ssend, srecv)
    s_ref[...] = s_total
    for q in range(2 * ORDER - 1):
        degree = abs(q - (ORDER - 1))
        sext_ref[q : q + 1] = s_ref[degree : degree + 1]
    lam = const_ref[3 * ORDER :, :LANES]
    sub = iota((ORDER, LANES), 0)
    system = []
    for b in range(ORDER):
        mean = 0.5 * (s_ref[b : b + ORDER] + sext_ref[ORDER - 1 - b : 2 * ORDER - 1 - b])
        system.append(lam * mean + jnp.where(sub == b, ridge_weight, 0.0))
    inverse = list(system)
    for k in range(ORDER):
        pivot = 1.0 / inverse[k][k : k + 1]
        off = jnp.where(sub == k, 0.0, inverse[k])
        for c in range(ORDER):
            if c != k:
                row = inverse[c][k : k + 1] * pivot
                inverse[c] = jnp.where(sub == k, row, inverse[c] - off * row)
        inverse[k] = jnp.where(sub == k, pivot, -off * pivot)

    def times(columns, x):
        total = columns[0] * x[0:1]
        for b in range(1, ORDER):
            total = total + columns[b] * x[b : b + 1]
        return total

    def solve(rhs):
        guess = times(inverse, rhs)
        return guess + times(inverse, rhs - times(system, guess))

    def by_term(coefs, fold):
        spread = jnp.concatenate([jnp.where(lane_visit == v, coefs, 0.0) for v in range(vis_local)], axis=0)
        return dot(fold, spread, NT, HIGH)

    for copy in sent_a:
        copy.wait_recv()
    arrived = pa_ref[...]
    for step in range(1, n_v):
        arrived = arrived + pa_recv[step]
    per_slot = 1.0 / (arrived[ORDER : ORDER + 1] + 1.0)
    projected = arrived[:ORDER] * per_slot
    m_recv[ci] = warped_moment - own_blocks(dot(design, repeat(projected), NT, HIGH))
    sent_b = over_ccd(m_recv, bsend, brecv)
    moment = total_over_ccd(m_recv, bsend, brecv)
    coefs = solve(moment)

    q_ref[...] = dot(by_term(coefs, const_ref[ORDER : 2 * ORDER, :LANES]), design, NN, HIGH)
    sent_c = over_visits(lambda step: q_ref, q_recv, csend, crecv)
    for copy in sent_c:
        copy.wait_recv()
    model = q_ref[...]
    for step in range(1, n_v):
        model = model + q_recv[step]
    m2_recv[ci] = lam * own_blocks(dot(design, repeat(model * per_slot), NT, HIGH))
    sent_d = over_ccd(m2_recv, dsend, drecv)

    mine = iota((P_DEV, npk), 1) == iota((P_DEV, npk), 0) + vi * P_DEV
    scale = jnp.where(mine, per_slot, 0.0)
    for copy in sent_g:
        copy.wait_recv()
    own = s1_ref[pl.ds(pl.multiple_of(vi * P_DEV, P_DEV), P_DEV)]
    for step in range(1, n_v):
        own = own + s1_recv[step]
    model_own = dot(dot(scale, model, NT, HIGH), cx, NN, HIGH)
    bg_ref[...] = own * jnp.sum(scale, axis=1, keepdims=True) - model_own

    moment = moment + total_over_ccd(m2_recv, dsend, drecv)
    off_ref[...] = by_term(solve(moment), const_ref[2 * ORDER : 3 * ORDER, :LANES])
    for copy in sent_s + sent_a + sent_b + sent_c + sent_d + sent_g:
        copy.wait_send()


def per_device(raw_rows, resample, slot_row, tap_weight, patch_id, live_mask):
    n_v, n_c = lax.axis_size("visit"), lax.axis_size("ccd")
    vis_local, rows, pixels = raw_rows.shape
    slots = slot_row.shape[3]
    npk, nvb = n_v * P_DEV, vis_local * ORDER
    consts = jnp.asarray(basis_constants(pixels, vis_local))
    vmem = pl.BlockSpec(memory_space=pltpu.VMEM)
    hbm = pl.BlockSpec(memory_space=pl.ANY)
    dma = pltpu.SemaphoreType.DMA
    coefs, background = pl.pallas_call(
        functools.partial(kernel, n_v, n_c, vis_local),
        out_shape=(
            jax.ShapeDtypeStruct((ORDER, nvb), F32),
            jax.ShapeDtypeStruct((P_DEV, pixels), F32),
        ),
        in_specs=[vmem] * 5 + [hbm] * 2,
        out_specs=(vmem, vmem),
        scratch_shapes=[
            pltpu.VMEM((vis_local, rows, pixels), BF16),
            pltpu.VMEM((vis_local, pixels, pixels), BF16),
            pltpu.VMEM((4, n_v, slots), jnp.int32),
            pltpu.VMEM((n_v, 2 * ORDER, slots), F32),
            pltpu.VMEM((vis_local, npk, rows), BF16),
            pltpu.VMEM((nvb, rows), F32),
            pltpu.VMEM((nvb, npk), F32),
            pltpu.VMEM((2 * ORDER, LANES), F32),
            pltpu.VMEM((2 * ORDER, LANES), F32),
            pltpu.VMEM((npk, pixels), F32),
            pltpu.VMEM((2 * ORDER, npk), F32),
            pltpu.VMEM((ORDER, npk), F32),
            pltpu.VMEM((n_c, 2 * ORDER, LANES), F32),
            pltpu.VMEM((n_c, ORDER, LANES), F32),
            pltpu.VMEM((n_c, ORDER, LANES), F32),
            pltpu.VMEM((n_v, 2 * ORDER, npk), F32),
            pltpu.VMEM((n_v, ORDER, npk), F32),
            pltpu.VMEM((n_v, P_DEV, pixels), F32),
            dma((2,)),
            dma((n_c,)), dma((n_c,)),
            dma((n_v,)), dma((n_v,)),
            dma((n_c,)), dma((n_c,)),
            dma((n_v,)), dma((n_v,)),
            dma((n_c,)), dma((n_c,)),
            dma((n_v,)), dma((n_v,)),
        ],
        compiler_params=pltpu.CompilerParams(
            collective_id=0, has_side_effects=True, vmem_limit_bytes=48 * 1024 * 1024
        ),
    )(slot_row[0, 0], tap_weight[:, 0, 0], patch_id[0, 0], live_mask[0, 0], consts, raw_rows, resample)
    offsets = coefs.reshape(ORDER, vis_local, ORDER).transpose(1, 0, 2).reshape(vis_local, ORDER * ORDER)
    return (offsets, background)


def solution(mesh):
    in_specs = (
        P("visit", "ccd", None),
        P("visit", None, None),
        P("visit", "ccd", None, None),
        P(None, "visit", "ccd", None, None),
        P("visit", "ccd", None, None),
        P("visit", "ccd", None, None),
    )
    out_specs = (P("visit", None), P(("visit", "ccd"), None))
    return jax.shard_map(
        per_device, mesh=mesh, in_specs=in_specs, out_specs=out_specs, check_vma=False
    )
```

time: 159 us -> 31.2 us (0.20)
  other arithmetic: 50.4 us -> 0 us
  blocking collectives: 46.2 us -> 0 us
  Pallas kernels: 0 us -> 23.1 us
  local copies, waits for them, and re-layouts: 23.7 us -> 6.96 us
  waiting for transfers between devices: 13.5 us -> 0 us
  starting transfers between devices: 12.8 us -> 0 us
  matrix products: 10.4 us -> 0 us
    another operation x8 -> x0, other arithmetic: 43.4 us -> none  [the longest x4 23.6 us: solve_offsets(): factor = jnp.linalg.cholesky(gram)]
    psum x2 -> x0, blocking collectives: 27.5 us -> none  [per_device(): design_total, moments = lax.psum((design_local, moments_local), 'ccd')]
    pallas_call x0 -> x1, Pallas kernels: none -> 23.1 us  [per_device(): pl.pallas_call(functools.partial(kernel, n_v, n_c, vis_local), out_shape=...]
    gather x8 -> x0, local copies, waits for them, and re-layouts: 22 us -> none  [the longest x4 16 us: per_device(): jnp.take(resampled, starts + tap_index, axis=0)]
    all_to_all x2 -> x0, blocking collectives: 18.7 us -> none  [the longest x1 9.35 us: per_device(): lax.all_to_all(returned, 'visit', split_axis=0, concat_axis=0, tiled=True)]
    all_to_all x3 -> x0, waiting for transfers between devices: 13.5 us -> none  [the longest x1 6.81 us: per_device(): lax.all_to_all(corrected, 'visit', split_axis=0, concat_axis=0, tiled=True)]
    all_to_all x3 -> x0, starting transfers between devices: 12.8 us -> none  [the longest x1 5.17 us: per_device(): lax.all_to_all(codes, 'visit', split_axis=0, concat_axis=0, tiled=True)]
    dot_general x12 -> x0, matrix products: 8.72 us -> none  [the longest x2 2.69 us: model_of(): jnp.einsum('...i,ip->...p', reduced, cheb_x, precision=lax.Precision.HIGH...]
  transfers between devices with their start and end apart: 3 -> 0, of which waited for: 2 -> 0; matrix products, arithmetic and copies ran while one was open for 18% -> 0% of each run, Pallas kernels for 0% -> 0%
where the time goes in v1:
time: 31.2 us; the launch traced here: 30.7 us
  Pallas kernels  23.1 us (74%)
  local copies, waits for them, and re-layouts  6.96 us (22%)
  between operations  0.66 us (2%)
    pallas_call x1, Pallas kernels, per_device(): pl.pallas_call(functools.partial(kernel, n_v, n_c, vis_local), out_shape=...  23.1 us
    unnamed x15, local copies, waits for them, and re-layouts  6.21 us
    reshape x2, local copies, waits for them, and re-layouts, per_device(): coefs.reshape(ORDER, vis_local, ORDER).transpose(1, 0, 2)  0.74 us

profile of v1, /device:TPU:0, one launch (start us, length us, event | category | flops | bytes accessed | tf_op | source)
XLA Modules:
  0.0 30.7 jit_solution(8124508571763050467)
XLA Ops:
  0.6 0.0 copy-start.4
  0.6 0.7 %copy-done.4 = s32[1,1,8,128]{3,2,1,0:T(8,128)S(1)} copy-done((s32[1,1,8,128]{3,2,1,0:T(8,128)S(1)}, s32[1,1,8,128]{3,2,1,0:T(8,128)}, u32[]{:S(2)}) %copy-start.4) | copy-done | bytes 4120
  1.3 0.0 copy-start
  1.3 1.2 %copy-done = bf16[4,1024,128]{2,1,0:T(8,128)(2,1)S(1)} copy-done((bf16[4,1024,128]{2,1,0:T(8,128)(2,1)S(1)}, bf16[4,1024,128]{2,1,0:T(8,128)(2,1)}, u32[]{:S(2)}) %copy-start) | copy-done | bytes 1048600
  2.5 0.0 copy-start.1
  2.5 0.9 %copy-done.1 = bf16[4,128,128]{2,1,0:T(8,128)(2,1)S(1)} copy-done((bf16[4,128,128]{2,1,0:T(8,128)(2,1)S(1)}, bf16[4,128,128]{2,1,0:T(8,128)(2,1)}, u32[]{:S(2)}) %copy-start.1) | copy-done | bytes 131096
  3.4 0.0 copy-start.2
  3.5 0.7 %copy-done.2 = f32[4,1,1,8,128]{4,3,2,1,0:T(8,128)S(1)} copy-done((f32[4,1,1,8,128]{4,3,2,1,0:T(8,128)S(1)}, f32[4,1,1,8,128]{4,3,2,1,0:T(8,128)}, u32[]{:S(2)}) %copy-start.2) | copy-done | bytes 16408
  4.2 0.0 copy-start.3
  4.2 0.7 %copy-done.3 = f32[32,128]{1,0:T(8,128)S(1)} copy-done((f32[32,128]{1,0:T(8,128)S(1)}, f32[32,128]{1,0:T(8,128)}, u32[]{:S(2)}) %copy-start.3) | copy-done | bytes 16408
  4.9 0.0 copy-start.5
  4.9 0.7 %copy-done.5 = s32[1,1,8,128]{3,2,1,0:T(8,128)S(1)} copy-done((s32[1,1,8,128]{3,2,1,0:T(8,128)S(1)}, s32[1,1,8,128]{3,2,1,0:T(8,128)}, u32[]{:S(2)}) %copy-start.5) | copy-done | bytes 4120
  5.6 0.0 copy-start.6
  5.6 0.7 %copy-done.6 = s32[1,1,8,128]{3,2,1,0:T(8,128)S(1)} copy-done((s32[1,1,8,128]{3,2,1,0:T(8,128)S(1)}, s32[1,1,8,128]{3,2,1,0:T(8,128)}, u32[]{:S(2)}) %copy-start.6) | copy-done | bytes 4120
  6.3 23.1 %shard_map.86 = (f32[8,32]{1,0:T(8,128)S(1)}, f32[16,128]{1,0:T(8,128)S(1)}) custom-call(s32[8,128]{1,0:T(8,128)S(1)} %bitcast.6, f32[4,8,128]{2,1,0:T(8,128)S(1)} %bitcast.5, s32[8,128]{1,0:T(8,128)S(1)} %bitcast.7, s32[8,128]{1,0:T(8,128)S(1)} %bitcast.8, f32[32,128]{1,0:T(8,128)S(1)} %copy-done.3, bf16[4,1024,128]{2,1,0:T(8,128)(2,1)S(1)} %copy-done, ...), custom_call_target="tpu_custom_call" | custom-call | tf_op jit(solution)/shard_map/pallas_call | solution.py:311
  29.4 0.1 reshape.10
  29.4 0.7 %reshape.11 = f32[4,64]{1,0:T(4,128)} reshape(f32[4,8,8]{2,1,0:T(8,128)S(1)} %copy.9) | data formatting | bytes 2048 | tf_op jit(solution)/shard_map/reshape | solution.py:350
  30.1 0.6 %copy.11 = f32[16,128]{1,0:T(8,128)} copy(f32[16,128]{1,0:T(8,128)S(1)} %get-tuple-element.9) | data formatting | bytes 16384
  (1 shorter events, 0.0 us)
Async XLA Ops:
  0.6 0.7 %copy-start.4 = (s32[1,1,8,128]{3,2,1,0:T(8,128)S(1)}, s32[1,1,8,128]{3,2,1,0:T(8,128)}, u32[]{:S(2)}) copy-start(s32[1,1,8,128]{3,2,1,0:T(8,128)} %param.9) | copy-start | bytes 12292
  1.3 1.2 %copy-start = (bf16[4,1024,128]{2,1,0:T(8,128)(2,1)S(1)}, bf16[4,1024,128]{2,1,0:T(8,128)(2,1)}, u32[]{:S(2)}) copy-start(bf16[4,1024,128]{2,1,0:T(8,128)(2,1)} %raw_hbm.1) | copy-start | bytes 3145732
  2.5 0.9 %copy-start.1 = (bf16[4,128,128]{2,1,0:T(8,128)(2,1)S(1)}, bf16[4,128,128]{2,1,0:T(8,128)(2,1)}, u32[]{:S(2)}) copy-start(bf16[4,128,128]{2,1,0:T(8,128)(2,1)} %res_hbm.1) | copy-start | bytes 393220
  3.4 0.7 %copy-start.2 = (f32[4,1,1,8,128]{4,3,2,1,0:T(8,128)S(1)}, f32[4,1,1,8,128]{4,3,2,1,0:T(8,128)}, u32[]{:S(2)}) copy-start(f32[4,1,1,8,128]{4,3,2,1,0:T(8,128)} %param.10) | copy-start | bytes 49156
  4.2 0.7 %copy-start.3 = (f32[32,128]{1,0:T(8,128)S(1)}, f32[32,128]{1,0:T(8,128)}, u32[]{:S(2)}) copy-start(f32[32,128]{1,0:T(8,128)} %constant.2.clone.const_ref) | copy-start | bytes 49156
  4.9 0.7 %copy-start.5 = (s32[1,1,8,128]{3,2,1,0:T(8,128)S(1)}, s32[1,1,8,128]{3,2,1,0:T(8,128)}, u32[]{:S(2)}) copy-start(s32[1,1,8,128]{3,2,1,0:T(8,128)} %param.11) | copy-start | bytes 12292
  5.6 0.7 %copy-start.6 = (s32[1,1,8,128]{3,2,1,0:T(8,128)S(1)}, s32[1,1,8,128]{3,2,1,0:T(8,128)}, u32[]{:S(2)}) copy-start(s32[1,1,8,128]{3,2,1,0:T(8,128)} %param.12) | copy-start | bytes 12292

commit v2 on v1

--- a/solution.py
+++ b/solution.py
@@ -16,7 +16,6 @@
 ridge_weight = 1.0
 
 MESH = pl.DeviceIdType.MESH
-HIGH = lax.Precision.HIGHEST
 F32 = jnp.float32
 BF16 = jnp.bfloat16
 NT = (((1,), (1,)), ((), ()))
@@ -56,21 +55,27 @@
     return out
 
 
+def wide_dot(a, b, dims):
+    a_head, a_tail = split(a, 2)
+    b_head, b_tail = split(b, 2)
+    return dot(a_head, b_head, dims) + (dot(a_head, b_tail, dims) + dot(a_tail, b_head, dims))
+
+
 def iota(shape, dim):
     return lax.broadcasted_iota(jnp.int32, shape, dim)
 
 
 def kernel(
     n_v, n_c, vis_local,
-    slot_ref, tap_ref, patch_ref, live_ref, const_ref, raw_hbm, res_hbm,
+    slot_hbm, tap_hbm, patch_hbm, live_hbm, const_hbm, raw_hbm, res_hbm,
     off_ref, bg_ref,
-    raw_ref, res_ref, iscr, tscr, wscr, tw_ref, d_ref, s_ref, sext_ref, s1_ref,
+    slot_ref, tap_ref, patch_ref, live_ref, const_ref, raw_ref, res_ref, iscr, tscr, wscr, tw_ref, d_ref, s_ref, sext_ref, s1_ref,
     pa_ref, q_ref, s_recv, m_recv, m2_recv, pa_recv, q_recv, s1_recv,
     load_sem, ssend, srecv, asend, arecv, bsend, brecv, csend, crecv, dsend, drecv, gsend, grecv,
 ):
     vi, ci = lax.axis_index("visit"), lax.axis_index("ccd")
     rows = raw_ref.shape[1]
-    slots = slot_ref.shape[1]
+    slots = slot_ref.shape[3]
     npk = n_v * P_DEV
     nvb = vis_local * ORDER
     v_peer = lambda step: (lax.rem(vi + step, n_v), ci)
@@ -81,10 +86,13 @@
         pl.semaphore_signal(barrier, inc=1, device_id=v_peer(step), device_id_type=MESH)
     for step in range(1, n_c):
         pl.semaphore_signal(barrier, inc=1, device_id=c_peer(step), device_id_type=MESH)
-    raw_load = pltpu.make_async_copy(raw_hbm, raw_ref, load_sem.at[0])
-    raw_load.start()
-    res_load = pltpu.make_async_copy(res_hbm, res_ref, load_sem.at[1])
-    res_load.start()
+    loads = []
+    for src, dst in (
+        (slot_hbm, slot_ref), (patch_hbm, patch_ref), (live_hbm, live_ref), (tap_hbm, tap_ref),
+        (raw_hbm, raw_ref), (res_hbm, res_ref), (const_hbm, const_ref),
+    ):
+        loads.append(pltpu.make_async_copy(src, dst, load_sem.at[len(loads)]))
+        loads[-1].start()
 
     def over_visits(src_of, dst, send, recv):
         copies = []
@@ -123,13 +131,15 @@
             total = total + buf[c]
         return total
 
-    start = slot_ref[...]
+    for load in loads[:4]:
+        load.wait()
+    start = slot_ref[0, 0]
     vis = jnp.zeros_like(start)
     for v in range(1, vis_local):
         vis = vis + (start >= v * rows).astype(jnp.int32)
     base = start - vis * rows
-    live = live_ref[...] > 0
-    patch = patch_ref[...]
+    live = live_ref[0, 0] > 0
+    patch = patch_ref[0, 0]
     iscr[0] = jnp.where(live, vis * P_DEV + patch, -1)
     iscr[1] = base
     iscr[2] = jnp.where(live, iota(start.shape, 0) * P_DEV + patch, -1)
@@ -143,56 +153,72 @@
     tw_ref[...] = jnp.zeros_like(tw_ref)
     d_ref[...] = jnp.zeros_like(d_ref)
     s_ref[...] = jnp.zeros_like(s_ref)
-    row_at = iota((ROW_BLOCK, slots), 0)
-
-    def chunk(j, carry):
-        at = pl.ds(j, 1)
-        first = iscr[1, at, :]
-        vis_j = iscr[3, at, :]
-        weights = [tap_ref[t, at, :] for t in range(TAPS)]
-        cheb = tscr[j]
-        hot = jnp.where(iota((vis_local * P_DEV, slots), 0) == iscr[0, at, :], 1.0, 0.0).astype(BF16)
-        cheb_v = jnp.concatenate(
-            [jnp.where(vis_j == v, cheb[:ORDER], 0.0) for v in range(vis_local)], axis=0
+    row_at = iota((ROW_BLOCK, slots), 0).astype(F32).astype(BF16)
+    group = 2 if n_v % 2 == 0 else 1
+    hots = vis_local * P_DEV
+
+    def chunk(step, carry):
+        tops, terms, marks = [], [], []
+        for part in range(group):
+            j = step * group + part
+            at = pl.ds(j, 1)
+            vis_j = iscr[3, at, :]
+            cheb = tscr[j]
+            hot = jnp.where(iota((hots, slots), 0) == iscr[0, at, :], 1.0, 0.0).astype(BF16)
+            cheb_v = jnp.concatenate(
+                [jnp.where(vis_j == v, cheb[:ORDER], 0.0) for v in range(vis_local)], axis=0
+            )
+            tv = split(cheb_v, 3)
+            empty = jnp.zeros_like(hot)
+            tops.append(jnp.concatenate([hot if p == part else empty for p in range(group)], axis=0))
+            terms.append(jnp.concatenate(tv[:2], axis=0))
+            first = iscr[1, at, :]
+            weights = [tap_ref[t, 0, 0, at, :].astype(BF16) for t in range(TAPS)]
+            marks.append((first, [jnp.broadcast_to(w, (ROW_BLOCK, slots)) for w in weights]))
+            member = jnp.where(iota((npk, slots), 0) == iscr[2, at, :], 1.0, 0.0).astype(BF16)
+            design = dot(jnp.concatenate(tv, axis=0), member, NT)
+            d_ref[...] += design[:nvb] + design[nvb : 2 * nvb] + design[2 * nvb :]
+            of_visit = jnp.where((iota((LANES, slots), 0) >> 3) == vis_j, 1.0, 0.0).astype(BF16)
+            sums = dot(jnp.concatenate(split(cheb, 3), axis=0), of_visit, NT)
+            s_ref[...] += sums[: 2 * ORDER] + sums[2 * ORDER : 4 * ORDER] + sums[4 * ORDER :]
+        lhs = jnp.concatenate(
+            [jnp.concatenate(tops, axis=1), jnp.concatenate(terms, axis=1)], axis=0
         )
-        tv = split(cheb_v, 3)
-        lhs = jnp.concatenate([hot, tv[0], tv[1]], axis=0)
-        hots = vis_local * P_DEV
         for block in range(0, rows, ROW_BLOCK):
-            gap = row_at - (first - block)
-            taps = jnp.zeros((ROW_BLOCK, slots), F32)
-            for t in range(TAPS):
-                taps = jnp.where(gap == t, weights[t], taps)
-            prod = dot(lhs, taps.astype(BF16), NT)
-            for v in range(vis_local):
-                wscr[v, pl.ds(pl.multiple_of(j * P_DEV, P_DEV), P_DEV), block : block + ROW_BLOCK] = (
-                    prod[v * P_DEV : (v + 1) * P_DEV].astype(BF16)
-                )
-            tw_ref[:, block : block + ROW_BLOCK] += prod[hots : hots + nvb] + prod[hots + nvb :]
-        member = jnp.where(iota((npk, slots), 0) == iscr[2, at, :], 1.0, 0.0).astype(BF16)
-        design = dot(jnp.concatenate(tv, axis=0), member, NT)
-        d_ref[...] += design[:nvb] + design[nvb : 2 * nvb] + design[2 * nvb :]
-        of_visit = jnp.where((iota((LANES, slots), 0) >> 3) == vis_j, 1.0, 0.0).astype(BF16)
-        sums = dot(jnp.concatenate(split(cheb, 3), axis=0), of_visit, NT)
-        s_ref[...] += sums[: 2 * ORDER] + sums[2 * ORDER : 4 * ORDER] + sums[4 * ORDER :]
+            wide = []
+            for first, weights in marks:
+                near = jnp.clip(first - block, -2 * TAPS, ROW_BLOCK + TAPS)
+                taps = jnp.zeros((ROW_BLOCK, slots), BF16)
+                for t in range(TAPS):
+                    taps = jnp.where(row_at == (near + t).astype(F32).astype(BF16), weights[t], taps)
+                wide.append(taps)
+            prod = dot(lhs, jnp.concatenate(wide, axis=1), NT)
+            for part in range(group):
+                at = pl.ds(pl.multiple_of((step * group + part) * P_DEV, P_DEV), P_DEV)
+                for v in range(vis_local):
+                    low = part * hots + v * P_DEV
+                    wscr[v, at, block : block + ROW_BLOCK] = prod[low : low + P_DEV].astype(BF16)
+            low = group * hots
+            tw_ref[:, block : block + ROW_BLOCK] += prod[low : low + nvb] + prod[low + nvb :]
         return carry
 
-    lax.fori_loop(0, n_v, chunk, 0)
+    lax.fori_loop(0, n_v // group, chunk, 0)
 
     pl.semaphore_wait(barrier, n_v + n_c - 2)
     s_recv[ci] = s_ref[...]
     sent_s = over_ccd(s_recv, ssend, srecv)
 
-    raw_load.wait()
-    res_load.wait()
-    tw = jnp.concatenate(split(tw_ref[...], 2), axis=0)
+    for load in loads[4:]:
+        load.wait()
     sums1 = jnp.zeros((npk, raw_ref.shape[2]), F32)
     row_sums = []
     for v in range(vis_local):
-        by_patch = dot(wscr[v], raw_ref[v], NN)
-        by_term = dot(tw, raw_ref[v], NN)
-        by_term = (by_term[:nvb] + by_term[nvb:])[v * ORDER : (v + 1) * ORDER]
-        mixed = jnp.concatenate([by_patch, by_term, jnp.zeros_like(by_term)], axis=0)
+        tw = tw_ref[v * ORDER : (v + 1) * ORDER]
+        tw_high = tw.astype(BF16).astype(F32)
+        tw = jnp.concatenate([tw_high, tw - tw_high], axis=0).astype(BF16)
+        by_patch = dot(jnp.concatenate([wscr[v], tw], axis=0), raw_ref[v], NN)
+        by_term = by_patch[npk : npk + ORDER] + by_patch[npk + ORDER :]
+        mixed = jnp.concatenate([by_patch[:npk], by_term, jnp.zeros_like(by_term)], axis=0)
         high, low = split(mixed, 2)
         warped = dot(high, res_ref[v], NN) + dot(low, res_ref[v], NN)
         sums1 = sums1 + warped[:npk]
@@ -203,7 +229,7 @@
     count = jnp.zeros((1, npk), F32)
     for v in range(vis_local):
         count = count + design[v * ORDER : v * ORDER + 1]
-    pa_ref[:ORDER] = dot(cx, sums1, NT, HIGH)
+    pa_ref[:ORDER] = wide_dot(cx, sums1, NT)
     pa_ref[ORDER:] = jnp.broadcast_to(count, (ORDER, npk))
     sent_a = over_visits(lambda step: pa_ref, pa_recv, asend, arecv)
 
@@ -224,7 +250,7 @@
     def repeat(x):
         return jnp.concatenate([x] * (LANES // ORDER), axis=0)
 
-    warped_moment = own_blocks(dot(jnp.concatenate(row_sums, axis=0), repeat(cx), NT, HIGH))
+    warped_moment = own_blocks(wide_dot(jnp.concatenate(row_sums, axis=0), repeat(cx), NT))
 
     s_total = total_over_ccd(s_recv, ssend, srecv)
     s_ref[...] = s_total
@@ -259,7 +285,7 @@
 
     def by_term(coefs, fold):
         spread = jnp.concatenate([jnp.where(lane_visit == v, coefs, 0.0) for v in range(vis_local)], axis=0)
-        return dot(fold, spread, NT, HIGH)
+        return wide_dot(fold, spread, NT)
 
     for copy in sent_a:
         copy.wait_recv()
@@ -268,19 +294,19 @@
         arrived = arrived + pa_recv[step]
     per_slot = 1.0 / (arrived[ORDER : ORDER + 1] + 1.0)
     projected = arrived[:ORDER] * per_slot
-    m_recv[ci] = warped_moment - own_blocks(dot(design, repeat(projected), NT, HIGH))
+    m_recv[ci] = warped_moment - own_blocks(wide_dot(design, repeat(projected), NT))
     sent_b = over_ccd(m_recv, bsend, brecv)
     moment = total_over_ccd(m_recv, bsend, brecv)
     coefs = solve(moment)
 
-    q_ref[...] = dot(by_term(coefs, const_ref[ORDER : 2 * ORDER, :LANES]), design, NN, HIGH)
+    q_ref[...] = wide_dot(by_term(coefs, const_ref[ORDER : 2 * ORDER, :LANES]), design, NN)
     sent_c = over_visits(lambda step: q_ref, q_recv, csend, crecv)
     for copy in sent_c:
         copy.wait_recv()
     model = q_ref[...]
     for step in range(1, n_v):
         model = model + q_recv[step]
-    m2_recv[ci] = lam * own_blocks(dot(design, repeat(model * per_slot), NT, HIGH))
+    m2_recv[ci] = lam * own_blocks(wide_dot(design, repeat(model * per_slot), NT))
     sent_d = over_ccd(m2_recv, dsend, drecv)
 
     mine = iota((P_DEV, npk), 1) == iota((P_DEV, npk), 0) + vi * P_DEV
@@ -290,7 +316,7 @@
     own = s1_ref[pl.ds(pl.multiple_of(vi * P_DEV, P_DEV), P_DEV)]
     for step in range(1, n_v):
         own = own + s1_recv[step]
-    model_own = dot(dot(scale, model, NT, HIGH), cx, NN, HIGH)
+    model_own = wide_dot(wide_dot(scale, model, NT), cx, NN)
     bg_ref[...] = own * jnp.sum(scale, axis=1, keepdims=True) - model_own
 
     moment = moment + total_over_ccd(m2_recv, dsend, drecv)
@@ -306,7 +332,7 @@
     npk, nvb = n_v * P_DEV, vis_local * ORDER
     consts = jnp.asarray(basis_constants(pixels, vis_local))
     vmem = pl.BlockSpec(memory_space=pltpu.VMEM)
-    hbm = pl.BlockSpec(memory_space=pl.ANY)
+    hbm = pl.BlockSpec(memory_space=pltpu.HBM)
     dma = pltpu.SemaphoreType.DMA
     coefs, background = pl.pallas_call(
         functools.partial(kernel, n_v, n_c, vis_local),
@@ -314,11 +340,16 @@
             jax.ShapeDtypeStruct((ORDER, nvb), F32),
             jax.ShapeDtypeStruct((P_DEV, pixels), F32),
         ),
-        in_specs=[vmem] * 5 + [hbm] * 2,
+        in_specs=[hbm] * 7,
         out_specs=(vmem, vmem),
         scratch_shapes=[
-            pltpu.VMEM((vis_local, rows, pixels), BF16),
-            pltpu.VMEM((vis_local, pixels, pixels), BF16),
+            pltpu.VMEM(slot_row.shape, jnp.int32),
+            pltpu.VMEM(tap_weight.shape, F32),
+            pltpu.VMEM(patch_id.shape, jnp.int32),
+            pltpu.VMEM(live_mask.shape, jnp.int32),
+            pltpu.VMEM(consts.shape, F32),
+            pltpu.VMEM(raw_rows.shape, BF16),
+            pltpu.VMEM(resample.shape, BF16),
             pltpu.VMEM((4, n_v, slots), jnp.int32),
             pltpu.VMEM((n_v, 2 * ORDER, slots), F32),
             pltpu.VMEM((vis_local, npk, rows), BF16),
@@ -335,7 +366,7 @@
             pltpu.VMEM((n_v, 2 * ORDER, npk), F32),
             pltpu.VMEM((n_v, ORDER, npk), F32),
             pltpu.VMEM((n_v, P_DEV, pixels), F32),
-            dma((2,)),
+            dma((7,)),
             dma((n_c,)), dma((n_c,)),
             dma((n_v,)), dma((n_v,)),
             dma((n_c,)), dma((n_c,)),
@@ -344,9 +375,9 @@
             dma((n_v,)), dma((n_v,)),
         ],
         compiler_params=pltpu.CompilerParams(
-            collective_id=0, has_side_effects=True, vmem_limit_bytes=48 * 1024 * 1024
+            collective_id=0, has_side_effects=True, vmem_limit_bytes=62 * 1024 * 1024
         ),
-    )(slot_row[0, 0], tap_weight[:, 0, 0], patch_id[0, 0], live_mask[0, 0], consts, raw_rows, resample)
+    )(slot_row, tap_weight, patch_id, live_mask, consts, raw_rows, resample)
     offsets = coefs.reshape(ORDER, vis_local, ORDER).transpose(1, 0, 2).reshape(vis_local, ORDER * ORDER)
     return (offsets, background)
 

time: 31.2 us -> 25.9 us (0.83)
  local copies, waits for them, and re-layouts: 6.96 us -> 2.06 us
    unnamed x15 -> x3, local copies, waits for them, and re-layouts: 6.21 us -> 0.63 us
    reshape x2, local copies, waits for them, and re-layouts: 0.74 us -> 1.42 us  [per_device(): coefs.reshape(ORDER, vis_local, ORDER).transpose(1, 0, 2)]
where the time goes in v2:
time: 25.9 us; the launch traced here: 25.6 us
  Pallas kernels  22.9 us (88%)
  local copies, waits for them, and re-layouts  2.06 us (8%)
  between operations  0.64 us (2%)
    pallas_call x1, Pallas kernels, per_device(): pl.pallas_call(functools.partial(kernel, n_v, n_c, vis_local), out_shape=...  22.9 us
    reshape x2, local copies, waits for them, and re-layouts, per_device(): coefs.reshape(ORDER, vis_local, ORDER).transpose(1, 0, 2)  1.42 us
    unnamed x3, local copies, waits for them, and re-layouts  0.63 us

profile of v2, /device:TPU:0, one launch (start us, length us, event | category | flops | bytes accessed | tf_op | source)
XLA Modules:
  0.0 25.6 jit_solution(10397344745837834030)
XLA Ops:
  0.6 22.9 %shard_map.86 = (f32[8,32]{1,0:T(8,128)}, f32[16,128]{1,0:T(8,128)}) custom-call(s32[1,1,8,128]{3,2,1,0:T(8,128)} %slot_hbm.1, f32[4,1,1,8,128]{4,3,2,1,0:T(8,128)} %tap_hbm.1, s32[1,1,8,128]{3,2,1,0:T(8,128)} %patch_hbm.1, s32[1,1,8,128]{3,2,1,0:T(8,128)} %live_hbm.1, f32[32,128]{1,0:T(8,128)} %constant.2.clone.const_hbm, bf16[4,1024,128]{2,1,0:T(8,128)(2,1)} %raw_hbm.1, ...), custom_call_target="tpu_custom_call" | custom-call | tf_op jit(solution)/shard_map/pallas_call | solution.py:337
  23.5 0.8 %reshape.10 = f32[8,4,8]{2,1,0:T(4,128)S(1)} reshape(f32[8,32]{1,0:T(8,128)} %get-tuple-element.4) | data formatting | bytes 2048 | tf_op jit(solution)/shard_map/reshape | solution.py:381
  24.3 0.0 copy-start
  24.3 0.7 %reshape.11 = f32[4,64]{1,0:T(4,128)} reshape(f32[4,8,8]{2,1,0:T(8,128)S(1)} %copy.9) | data formatting | bytes 2048 | tf_op jit(solution)/shard_map/reshape | solution.py:381
  24.9 0.0 copy-done
  25.0 0.6 %copy.11 = f32[16,128]{1,0:T(8,128)} copy(f32[16,128]{1,0:T(8,128)S(1)} %copy-done) | data formatting | bytes 16384
  (1 shorter events, 0.0 us)
Async XLA Ops:
  24.3 0.7 %copy-start = (f32[16,128]{1,0:T(8,128)S(1)}, f32[16,128]{1,0:T(8,128)}, u32[]{:S(2)}) copy-start(f32[16,128]{1,0:T(8,128)} %get-tuple-element.9) | copy-start | bytes 24580
